TPU v7x, 32 devices: a whole 2x2x4 slice. The times are simulated.
32 devices in a mesh: mol: 2 (over x), occ: 16 (over z, y, core).
Axes of the slice: x: 2, y: 2, z: 4, core: 2. Of those that a mesh axis runs over, the one named last changes fastest.
Arguments:
- amplitudes: bfloat16 [256, 16, 64, 64], P(('mol', 'occ')), parts along dimension 0, may hold values from -0.16699219 to 0.16699219
- lambdas: bfloat16 [256, 16, 64, 64], P(('mol', 'occ')), parts along dimension 0, may hold values from -6 to 6
- pair_list: int32 [256, 2], P(('mol', 'occ')), parts along dimension 0, may hold values from 0 to 299
- tile_list: int32 [16, 2], replicated, may hold values from 0 to 37
- occ_energy: float32 [600], P('mol'), parts along dimension 0, may hold values from -2 to -0.5
- vir_energy: float32 [4864], P('mol'), parts along dimension 0, may hold values from 0.5 to 3
Outputs:
- new_lambdas: bfloat16 [256, 16, 64, 64], P(('mol', 'occ')), parts along dimension 0
There are 2 independent parts, one for each index of `mol`. A program takes and returns all parts, laid end to end along the dimension named above; an argument that names none is the same for every part. Nothing has to cross between parts.
All inputs are finite; a program needn't handle non-finite values.
Results may differ from a plain program's by a relative error of at most 0.0075.
Values may be sent and summed in bfloat16 or wider, within the bound.
A program may use at most 128 MiB of HBM per device.

v0:
```python
import jax
import jax.numpy as jnp
from jax import lax
from jax.sharding import PartitionSpec as P


def select_rows(table, indices):
    picks = (indices[:, None] == jnp.arange(table.shape[0], dtype=jnp.int32)[None, :]).astype(
        jnp.float32
    )
    return jnp.dot(picks, table, precision=lax.Precision.HIGHEST)


def finish_update(lam_part, ladder_part, pairs, tiles, occ_energy, vir_energy):
    tile_size = lam_part.shape[2]
    vir_tiles = vir_energy.reshape(-1, tile_size)
    first_vir = select_rows(vir_tiles, tiles[:, 0])
    second_vir = select_rows(vir_tiles, tiles[:, 1])
    occ_column = occ_energy[:, None]
    occ_first = select_rows(occ_column, pairs[:, 0])[:, 0]
    occ_second = select_rows(occ_column, pairs[:, 1])[:, 0]
    denom = (
        first_vir[None, :, :, None]
        + second_vir[None, :, None, :]
        - occ_first[:, None, None, None]
        - occ_second[:, None, None, None]
    )
    total = lam_part.astype(jnp.float32) + ladder_part.astype(jnp.float32)
    return (total / denom).astype(jnp.bfloat16)


def shards(amplitudes, lambdas, pair_list, tile_list, occ_energy, vir_energy):
    amp_tiles, lam_tiles = (
        lax.all_to_all(amplitudes, "occ", split_axis=1, concat_axis=0, tiled=True),
        lax.all_to_all(lambdas, "occ", split_axis=1, concat_axis=0, tiled=True),
    )
    all_pairs = amp_tiles.shape[0]
    amp_flat = amp_tiles.reshape(all_pairs, -1)
    lam_flat = lam_tiles.reshape(all_pairs, -1)
    partial_intersection = lax.dot_general(
        amp_flat, lam_flat, (((1,), (1,)), ((), ())), preferred_element_type=jnp.float32
    )
    intersection = lax.psum(partial_intersection, "occ")
    intersection_b = intersection.astype(jnp.bfloat16)
    ladder = (0.5 * jnp.dot(intersection_b, amp_flat, preferred_element_type=jnp.float32)).astype(
        jnp.bfloat16
    )
    ladder = ladder.reshape(amp_tiles.shape)
    ladder_home = lax.all_to_all(ladder, "occ", split_axis=0, concat_axis=1, tiled=True)
    return finish_update(lambdas, ladder_home, pair_list, tile_list, occ_energy, vir_energy)


def solution(mesh):
    return jax.shard_map(
        shards,
        mesh=mesh,
        in_specs=(
            P(("mol", "occ"), None, None, None),
            P(("mol", "occ"), None, None, None),
            P(("mol", "occ"), None),
            P(),
            P("mol"),
            P("mol"),
        ),
        out_specs=P(("mol", "occ"), None, None, None),
        check_vma=False,
    )
```

profile of v0, /device:TPU:0, one launch (start us, length us, event | category | flops | bytes accessed | tf_op | source)
XLA Modules:
  0.0 180.0 jit_solution(15488987364868504580)
XLA Ops:
  0.0 3.1 %copy.23 = bf16[8,16,64,64]{3,2,0,1:T(8,128)(2,1)} copy(bf16[8,16,64,64]{3,2,1,0:T(8,128)(2,1)} %param.6) | data formatting | bytes 2097152 | tf_op args[0]
  3.2 4.8 %reshape.46 = bf16[16,2,16384]{2,1,0:T(2,128)(2,1)} reshape(bf16[16,8,64,64]{3,2,1,0:T(8,128)(2,1)} %bitcast.60) | data formatting | bytes 2097152
  7.9 7.4 %all-to-all-start = ((bf16[16,2,16384]{2,1,0:T(2,128)(2,1)}), bf16[16,2,16384]{2,1,0:T(2,128)(2,1)S(1)}, u32[]{:S(2)}, u32[]{:S(2)}) async-start(bf16[16,2,16384]{2,1,0:T(2,128)(2,1)} %reshape.46), calls=%async_computation | async-start | bytes 2097152 | tf_op jit(solution)/shard_map/all_to_all | solution.py:34
  15.3 1.6 copy.24
  16.9 4.6 %reshape.48 = bf16[16,2,16384]{2,1,0:T(2,128)(2,1)} reshape(bf16[16,8,64,64]{3,2,1,0:T(8,128)(2,1)} %bitcast.61) | data formatting | bytes 2097152
  21.5 16.7 %all-to-all-done = bf16[16,2,16384]{2,1,0:T(2,128)(2,1)S(1)} async-done(((bf16[16,2,16384]{2,1,0:T(2,128)(2,1)}), bf16[16,2,16384]{2,1,0:T(2,128)(2,1)S(1)}, u32[]{:S(2)}, u32[]{:S(2)}) %all-to-all-start) | async-done | bytes 1048608 | tf_op jit(solution)/shard_map/all_to_all | solution.py:34
  38.3 6.9 %all-to-all-start.1 = ((bf16[16,2,16384]{2,1,0:T(2,128)(2,1)}), bf16[16,2,16384]{2,1,0:T(2,128)(2,1)}, u32[]{:S(2)}, u32[]{:S(2)}) async-start(bf16[16,2,16384]{2,1,0:T(2,128)(2,1)} %reshape.48), calls=%async_computation.1 | async-start | bytes 2097152 | tf_op jit(solution)/shard_map/all_to_all | solution.py:35
  45.2 1.3 reshape.47
  46.5 1.6 bitcast_bitcast_fusion.1
  48.1 3.3 %reshape.36 = bf16[128,4096]{1,0:T(8,128)(2,1)S(1)} reshape(bf16[16,8,1,64,64]{4,3,1,0,2:T(8,128)(2,1)} %bitcast_bitcast_fusion.1) | data formatting | bytes 2097152 | tf_op jit(solution)/shard_map/reshape | solution.py:38
  51.5 16.7 %all-to-all-done.1 = bf16[16,2,16384]{2,1,0:T(2,128)(2,1)} async-done(((bf16[16,2,16384]{2,1,0:T(2,128)(2,1)}), bf16[16,2,16384]{2,1,0:T(2,128)(2,1)}, u32[]{:S(2)}, u32[]{:S(2)}) %all-to-all-start.1) | async-done | bytes 1048608 | tf_op jit(solution)/shard_map/all_to_all | solution.py:35
  68.2 3.8 %reshape.49 = bf16[16,8,64,64]{3,2,1,0:T(8,128)(2,1)S(1)} reshape(bf16[16,2,16384]{2,1,0:T(2,128)(2,1)} %all-to-all-done.1) | data formatting | bytes 2097152
  72.0 1.6 bitcast_bitcast_fusion
  73.5 3.3 %reshape.37 = bf16[128,4096]{1,0:T(8,128)(2,1)S(1)} reshape(bf16[16,8,1,64,64]{4,3,1,0,2:T(8,128)(2,1)} %bitcast_bitcast_fusion) | data formatting | bytes 2097152 | tf_op jit(solution)/shard_map/reshape | solution.py:39
  76.9 0.4 fusion.10
  77.3 63.0 %psum.7 = bf16[128,128]{1,0:T(8,128)(2,1)S(1)} all-reduce(f32[128,128]{1,0:T(8,128)S(1)} %fusion.10), channel_id=1, replica_groups=mesh['mol'=2,'occ'=16] {'occ'}, use_global_device_ids=true, to_apply=%region_0.0 | all-reduce | flops 16384 | bytes 98304 | tf_op jit(solution)/shard_map/psum | solution.py:43
  140.3 0.4 fusion
  140.7 0.7 copy.16
  141.4 3.0 %copy.17 = bf16[128,1,64,64]{3,2,1,0:T(8,128)(2,1)S(1)} copy(bf16[128,1,64,64]{0,3,2,1:T(8,128)(2,1)S(1)} %bitcast.62) | data formatting | bytes 2097152 | tf_op jit(solution)/shard_map/reshape | solution.py:48
  144.4 0.0 copy-start.4
  144.4 2.2 %reshape.50 = bf16[16,2,16384]{2,1,0:T(2,128)(2,1)} reshape(bf16[128,1,64,64]{3,2,1,0:T(8,128)(2,1)S(1)} %copy.17) | data formatting | bytes 2097152
  146.7 3.7 %all-to-all-start.2 = ((bf16[16,2,16384]{2,1,0:T(2,128)(2,1)}), bf16[16,2,16384]{2,1,0:T(2,128)(2,1)S(1)}, u32[]{:S(2)}, u32[]{:S(2)}) async-start(bf16[16,2,16384]{2,1,0:T(2,128)(2,1)} %reshape.50), calls=%async_computation.2 | async-start | bytes 2097152 | tf_op jit(solution)/shard_map/all_to_all | solution.py:49
  150.4 0.1 reshape.39
  150.5 0.2 convolution_bitcast_fusion
  150.7 0.2 convolution_bitcast_fusion.1
  150.9 0.2 fusion.5
  151.1 0.2 fusion.4
  151.3 1.0 broadcast_add_fusion
  152.3 21.0 %all-to-all-done.2 = bf16[16,2,16384]{2,1,0:T(2,128)(2,1)S(1)} async-done(((bf16[16,2,16384]{2,1,0:T(2,128)(2,1)}), bf16[16,2,16384]{2,1,0:T(2,128)(2,1)S(1)}, u32[]{:S(2)}, u32[]{:S(2)}) %all-to-all-start.2) | async-done | bytes 1048608 | tf_op jit(solution)/shard_map/all_to_all | solution.py:49
  173.3 2.3 %reshape.51 = bf16[128,1,64,64]{3,2,1,0:T(8,128)(2,1)} reshape(bf16[16,2,16384]{2,1,0:T(2,128)(2,1)S(1)} %all-to-all-done.2) | data formatting | bytes 2097152
  175.6 2.8 %fusion.2 = bf16[8,16,64,64]{3,2,0,1:T(8,128)(2,1)S(1)} fusion(bf16[16,8,1,64,64]{4,3,1,0,2:T(8,128)(2,1)} %bitcast.59, f32[8]{0:T(128)S(1)} %convolution_bitcast_fusion, f32[8]{0:T(128)S(1)} %convolution_bitcast_fusion.1, f32[16,64,64]{2,1,0:T(8,128)} %broadcast_add_fusion, bf16[8,16,64,64]{3,2,1,0:T(8,128)(2,1)S(1)} %copy-done.1), kind=kLoop, calls=%fused_computation.4 | loop fusion | flops 3670016 | bytes 3407936 | tf_op jit(solution)/shard_map/convert_element_type | solution.py:29
  178.4 1.6 copy.19
  (14 shorter events, 0.1 us)
Async XLA Ops:
  3.2 12.2 %copy-start = (bf16[8,16,64,64]{3,2,1,0:T(8,128)(2,1)S(1)}, bf16[8,16,64,64]{3,2,1,0:T(8,128)(2,1)}, u32[]{:S(2)}) copy-start(bf16[8,16,64,64]{3,2,1,0:T(8,128)(2,1)} %param.7) | copy-start | bytes 3145732
  7.9 30.3 %all-to-all-start = ((bf16[16,2,16384]{2,1,0:T(2,128)(2,1)}), bf16[16,2,16384]{2,1,0:T(2,128)(2,1)S(1)}, u32[]{:S(2)}, u32[]{:S(2)}) async-start(bf16[16,2,16384]{2,1,0:T(2,128)(2,1)} %reshape.46), calls=%async_computation | async-start | bytes 2097152 | tf_op jit(solution)/shard_map/all_to_all | solution.py:34
  38.3 29.9 %all-to-all-start.1 = ((bf16[16,2,16384]{2,1,0:T(2,128)(2,1)}), bf16[16,2,16384]{2,1,0:T(2,128)(2,1)}, u32[]{:S(2)}, u32[]{:S(2)}) async-start(bf16[16,2,16384]{2,1,0:T(2,128)(2,1)} %reshape.48), calls=%async_computation.1 | async-start | bytes 2097152 | tf_op jit(solution)/shard_map/all_to_all | solution.py:35
  144.4 6.0 %copy-start.3 = (f32[300]{0:T(512)S(1)}, f32[300]{0:T(512)}, u32[]{:S(2)}) copy-start(f32[300]{0:T(512)} %param.10) | copy-start | bytes 3604
  144.4 6.0 %copy-start.2 = (f32[2432]{0:T(1024)S(1)}, f32[2432]{0:T(1024)}, u32[]{:S(2)}) copy-start(f32[2432]{0:T(1024)} %param.11) | copy-start | bytes 29188
  144.4 6.1 %copy-start.4 = (s32[8,2]{0,1:T(2,128)S(1)}, s32[8,2]{0,1:T(2,128)}, u32[]{:S(2)}) copy-start(s32[8,2]{0,1:T(2,128)} %param.8) | copy-start | bytes 196
  144.4 6.4 %copy-start.5 = (s32[16,2]{0,1:T(2,128)S(1)}, s32[16,2]{0,1:T(2,128)}, u32[]{:S(2)}) copy-start(s32[16,2]{0,1:T(2,128)} %param.9) | copy-start | bytes 388
  146.7 26.6 %all-to-all-start.2 = ((bf16[16,2,16384]{2,1,0:T(2,128)(2,1)}), bf16[16,2,16384]{2,1,0:T(2,128)(2,1)S(1)}, u32[]{:S(2)}, u32[]{:S(2)}) async-start(bf16[16,2,16384]{2,1,0:T(2,128)(2,1)} %reshape.50), calls=%async_computation.2 | async-start | bytes 2097152 | tf_op jit(solution)/shard_map/all_to_all | solution.py:49
  150.4 25.2 %copy-start.1 = (bf16[8,16,64,64]{3,2,1,0:T(8,128)(2,1)S(1)}, bf16[8,16,64,64]{3,2,1,0:T(8,128)(2,1)}, u32[]{:S(2)}) copy-start(bf16[8,16,64,64]{3,2,1,0:T(8,128)(2,1)} %param.7) | copy-start | bytes 3145732
where the time goes:
time: 182 us; the launch traced here: 180 us
  blocking collectives  63 us (35%)
  waiting for transfers between devices  54.4 us (30%)
  local copies, waits for them, and re-layouts  38.9 us (21%)
  starting transfers between devices  18 us (10%)
  other arithmetic  3.86 us (2%)
    psum x1, blocking collectives, shards(): intersection = lax.psum(partial_intersection, 'occ')  63 us
    unnamed x21, local copies, waits for them, and re-layouts  23.8 us
    all_to_all x1, waiting for transfers between devices, shards(): lax.all_to_all(ladder, 'occ', split_axis=0, concat_axis=1, tiled=True)  21 us
    all_to_all x1, waiting for transfers between devices, shards(): lax.all_to_all(amplitudes, 'occ', split_axis=1, concat_axis=0, tiled=True)  16.7 us
    all_to_all x1, waiting for transfers between devices, shards(): lax.all_to_all(lambdas, 'occ', split_axis=1, concat_axis=0, tiled=True)  16.7 us
    all_to_all x1, starting transfers between devices, shards(): lax.all_to_all(amplitudes, 'occ', split_axis=1, concat_axis=0, tiled=True)  7.39 us
    all_to_all x1, starting transfers between devices, shards(): lax.all_to_all(lambdas, 'occ', split_axis=1, concat_axis=0, tiled=True)  6.92 us
    all_to_all x1, starting transfers between devices, shards(): lax.all_to_all(ladder, 'occ', split_axis=0, concat_axis=1, tiled=True)  3.66 us
  transfers between devices with their start and end apart: 3, of which 3 were waited for; matrix products, arithmetic and copies ran while one was open for 8% of the time, Pallas kernels for 0%

commit v1 on v0

v1 whole, which is shorter than its diff:
```python
import functools

import jax
import jax.numpy as jnp
from jax import lax
from jax.experimental import pallas as pl
from jax.experimental.pallas import tpu as pltpu
from jax.sharding import PartitionSpec as P

F32 = jnp.float32
BF16 = jnp.bfloat16
HELD = 8
ROWS = 256
FOLD = 32


def fold_tile(x):
    return jnp.concatenate([x[:, :FOLD, :], x[:, FOLD:, :]], axis=-1)


def kernel(
    n, groups, nt,
    tiles_ref, pairs_ref, occ_ref, vir_ref, amp_hbm, lam_hbm,
    out_hbm,
    amp, lam, pt, plam, lamh, tbuf, lbuf, lad, ladr, dscr, gacc, asend, arecv, bsend, brecv, kmat,
    in_sem, t_send, t_recv, l_send, l_recv, a_send, a_recv, b_send, b_recv, d_send, d_recv, o_sem,
):
    cols = n // groups
    per = nt // cols
    me = lax.axis_index("occ")
    c = me % cols
    first = (me // cols) * cols

    def chunk(k):
        return lax.rem(c + k, cols)

    def load(which, src, dst, cc):
        span = pl.ds(cc * per, per)
        return pltpu.make_async_copy(src.at[:, span], dst.at[:, span], in_sem.at[which, cc])

    def load_start(k, _):
        load(0, amp_hbm, amp, chunk(k)).start()
        load(1, lam_hbm, lam, chunk(k)).start()
        return 0

    lax.fori_loop(0, cols, load_start, 0)

    barrier = pltpu.get_barrier_semaphore()

    def greet(k, _):
        pl.semaphore_signal(
            barrier, inc=1, device_id={"occ": lax.rem(me + k, n)}, device_id_type=pl.DeviceIdType.MESH
        )
        return 0

    lax.fori_loop(1, n, greet, 0)

    r_id = lax.broadcasted_iota(jnp.int32, (ROWS, ROWS), 0)
    m_id = lax.broadcasted_iota(jnp.int32, (ROWS, ROWS), 1)
    pack_m = ((r_id % HELD) * FOLD + r_id // HELD == m_id).astype(BF16)
    unpack_m = ((m_id % HELD) * FOLD + m_id // HELD == r_id).astype(BF16)

    def pack(cc):
        load(0, amp_hbm, amp, cc).wait()
        load(1, lam_hbm, lam, cc).wait()
        for i in range(per):
            s = cc * per + i
            t = fold_tile(amp[:, s]).reshape(ROWS, 2 * 64)
            pt[s] = jnp.dot(pack_m, t, preferred_element_type=F32).astype(BF16)
            u = fold_tile(lam[:, s]).reshape(ROWS, 2 * 64)
            lamh[s] = u
            plam[s] = jnp.dot(pack_m, u, preferred_element_type=F32).astype(BF16)

    def rcopy(src, dst, send, recv, peer):
        return pltpu.make_async_remote_copy(
            src_ref=src, dst_ref=dst, send_sem=send, recv_sem=recv,
            device_id={"occ": peer}, device_id_type=pl.DeviceIdType.MESH,
        )

    def send_t(peer):
        span = pl.ds(lax.rem(peer, cols) * per, per)
        return rcopy(pt.at[span], tbuf.at[me], t_send.at[peer], t_recv.at[me], peer)

    def send_l(cc):
        return rcopy(plam.at[pl.ds(cc * per, per)], lbuf.at[c], l_send.at[cc], l_recv.at[c], first + cc)

    def wait_t(src):
        rcopy(pt.at[pl.ds(0, per)], tbuf.at[src], t_send.at[src], t_recv.at[src], src).wait_recv()

    def wait_l(cc):
        rcopy(plam.at[pl.ds(0, per)], lbuf.at[cc], l_send.at[cc], l_recv.at[cc], first + cc).wait_recv()

    pack(c)
    pl.semaphore_wait(barrier, n - 1)
    for g in range(1, groups):
        send_t(lax.rem(me + g * cols, n)).start()

    def pack_send(k, _):
        cc = chunk(k)
        pack(cc)
        for g in range(groups - 1, -1, -1):
            send_t(lax.rem(first + g * cols, n) + cc).start()
        send_l(cc).start()
        return 0

    lax.fori_loop(1, cols, pack_send, 0)
    tbuf[me] = pt[pl.ds(c * per, per)]
    lbuf[c] = plam[pl.ds(c * per, per)]

    def energies(s, _):
        one = vir_ref[pl.ds(tiles_ref[s, 0], 1), :]
        two = vir_ref[pl.ds(tiles_ref[s, 1], 1), :]
        d = jnp.transpose(jnp.broadcast_to(one, (64, 64))) + two
        dscr[s] = jnp.concatenate([d[:FOLD], d[FOLD:]], axis=-1)
        return 0

    lax.fori_loop(0, nt, energies, 0)

    def arrive_t(k, _):
        wait_t(lax.rem(me + n - k, n))
        return 0

    def arrive_l(k, _):
        wait_l(lax.rem(c + cols - k, cols))
        return 0

    lax.fori_loop(1, cols, arrive_l, 0)
    lax.fori_loop(1, n, arrive_t, 0)

    def two_rows(ref, lo, count, t, g):
        a = ref[pl.ds(lo, count), t, pl.ds(g * 32, 16), :].reshape(count * 16, 128)
        b = ref[pl.ds(lo, count), t, pl.ds(g * 32 + 16, 16), :].reshape(count * 16, 128)
        return jnp.concatenate([a, b], axis=-1)

    gacc[...] = jnp.zeros_like(gacc)
    for t in range(per):
        def gram(g, _):
            y = two_rows(lbuf, 0, cols, t, g)
            for lo in range(0, n, 16):
                x = two_rows(tbuf, lo, 16, t, g)
                gacc[pl.ds(lo * 16, 256), :] += lax.dot_general(
                    x, y, (((1,), (1,)), ((), ())), preferred_element_type=F32
                )
            return 0

        lax.fori_loop(0, ROWS // 32, gram, 0, unroll=4 if n <= 16 else 1)

    width = cols * 16
    odd = (lax.broadcasted_iota(jnp.int32, (HELD, width), 1) // HELD) % 2

    def fold_gram(i, _):
        lo = gacc[pl.ds(i * 16, HELD), :]
        hi = gacc[pl.ds(i * 16 + HELD, HELD), :]
        asend[i] = jnp.where(odd == 0, lo, hi)
        return 0

    lax.fori_loop(0, n, fold_gram, 0, unroll=4)

    def send_a(peer):
        return rcopy(asend.at[peer], arecv.at[me], a_send.at[peer], a_recv.at[me], peer)

    def start_a(k, _):
        send_a(lax.rem(me + k, n)).start()
        return 0

    lax.fori_loop(1, n, start_a, 0)
    arecv[me] = asend[me]

    def arrive_a(k, _):
        src = lax.rem(me + n - k, n)
        rcopy(asend.at[src], arecv.at[src], a_send.at[src], a_recv.at[src], src).wait_recv()
        return 0

    lax.fori_loop(1, n, arrive_a, 0)
    for g in range(groups):
        total = arecv[g * cols]
        for i in range(1, cols):
            total = total + arecv[g * cols + i]
        other = jnp.where(odd == 0, pltpu.roll(total, width - HELD, 1), pltpu.roll(total, HELD, 1))
        rounded = (total + other).astype(BF16).astype(F32)
        bsend[:, g * width:(g + 1) * width] = 0.5 * rounded

    def send_b(cc):
        return rcopy(bsend, brecv.at[c], b_send.at[cc], b_recv.at[c], first + cc)

    def start_b(k, _):
        send_b(chunk(k)).start()
        return 0

    lax.fori_loop(1, cols, start_b, 0)
    brecv[c] = bsend[...]

    def arrive_b(k, _):
        cc = lax.rem(c + cols - k, cols)
        rcopy(bsend, brecv.at[cc], b_send.at[cc], b_recv.at[cc], first + cc).wait_recv()
        return 0

    lax.fori_loop(1, cols, arrive_b, 0)
    all_odd = (lax.broadcasted_iota(jnp.int32, (HELD, n * 16), 1) // HELD) % 2

    def expand(i, _):
        rows = brecv[i]
        both = jnp.concatenate(
            [jnp.where(all_odd == 0, rows, 0.0), jnp.where(all_odd == 1, rows, 0.0)], axis=0
        )
        kmat[pl.ds(i * 16, 16), :] = both.astype(BF16)
        return 0

    lax.fori_loop(0, cols, expand, 0, unroll=4)

    def send_d(cc, t):
        return rcopy(lad.at[cc, t], ladr.at[c, t], d_send.at[cc, t], d_recv.at[c, t], first + cc)

    for t in range(per):
        def ladder(g, _):
            x = two_rows(tbuf, 0, n, t, g)
            y = jnp.dot(kmat[...], x, preferred_element_type=F32).astype(BF16)
            lad[:, t, pl.ds(g * 32, 16), :] = y[:, :128].reshape(cols, 16, 128)
            lad[:, t, pl.ds(g * 32 + 16, 16), :] = y[:, 128:].reshape(cols, 16, 128)
            return 0

        lax.fori_loop(0, ROWS // 32, ladder, 0, unroll=4 if n <= 16 else 1)

        def start_d(k, _):
            send_d(chunk(k), t).start()
            return 0

        lax.fori_loop(1, cols, start_d, 0)
    ladr[c] = lad[c]

    def store(cc):
        span = pl.ds(cc * per, per)
        return pltpu.make_async_copy(amp.at[:, span], out_hbm.at[:, span], o_sem.at[cc])

    def finish(cc):
        for t in range(per):
            s = cc * per + t
            z = jnp.dot(unpack_m, ladr[cc, t], preferred_element_type=F32)
            total = lamh[s].astype(F32) + z
            d = dscr[s]
            for p in range(HELD):
                e = d - occ_ref[pairs_ref[p, 0]] - occ_ref[pairs_ref[p, 1]]
                q = total[p * FOLD:(p + 1) * FOLD] / e
                amp[p, s, :FOLD, :] = q[:, :64].astype(BF16)
                amp[p, s, FOLD:, :] = q[:, 64:].astype(BF16)
        store(cc).start()

    finish(c)

    def arrive_d(k, _):
        cc = lax.rem(c + cols - k, cols)
        for t in range(per):
            rcopy(
                lad.at[cc, t], ladr.at[cc, t], d_send.at[cc, t], d_recv.at[cc, t], first + cc
            ).wait_recv()
        finish(cc)
        return 0

    lax.fori_loop(1, cols, arrive_d, 0)

    def drain_n(k, _):
        peer = lax.rem(me + k, n)
        send_t(peer).wait_send()
        send_a(peer).wait_send()
        return 0

    lax.fori_loop(1, n, drain_n, 0)

    def drain_c(k, _):
        cc = chunk(k)
        send_l(cc).wait_send()
        send_b(cc).wait_send()
        for t in range(per):
            send_d(cc, t).wait_send()
        return 0

    lax.fori_loop(1, cols, drain_c, 0)

    def drain_out(k, _):
        store(k).wait()
        return 0

    lax.fori_loop(0, cols, drain_out, 0)


def shards(n, amplitudes, lambdas, pair_list, tile_list, occ_energy, vir_energy):
    nt = amplitudes.shape[1]
    groups = 2
    cols = n // groups
    per = nt // cols
    packed = (nt, ROWS, 128)
    dma = pltpu.SemaphoreType.DMA
    smem = pl.BlockSpec(memory_space=pltpu.SMEM)
    vmem = pl.BlockSpec(memory_space=pltpu.VMEM)
    hbm = pl.BlockSpec(memory_space=pl.ANY)
    return pl.pallas_call(
        functools.partial(kernel, n, groups, nt),
        out_shape=jax.ShapeDtypeStruct(lambdas.shape, BF16),
        in_specs=[smem, smem, smem, vmem, hbm, hbm],
        out_specs=hbm,
        scratch_shapes=[
            pltpu.VMEM(amplitudes.shape, BF16),
            pltpu.VMEM(lambdas.shape, BF16),
            pltpu.VMEM(packed, BF16),
            pltpu.VMEM(packed, BF16),
            pltpu.VMEM(packed, BF16),
            pltpu.VMEM((n, per, ROWS, 128), BF16),
            pltpu.VMEM((cols, per, ROWS, 128), BF16),
            pltpu.VMEM((cols, per, ROWS, 128), BF16),
            pltpu.VMEM((cols, per, ROWS, 128), BF16),
            pltpu.VMEM((nt, FOLD, 128), F32),
            pltpu.VMEM((n * 16, cols * 16), F32),
            pltpu.VMEM((n, HELD, cols * 16), F32),
            pltpu.VMEM((n, HELD, cols * 16), F32),
            pltpu.VMEM((HELD, n * 16), F32),
            pltpu.VMEM((cols, HELD, n * 16), F32),
            pltpu.VMEM((cols * 16, n * 16), BF16),
            dma((2, cols)),
            dma((n,)), dma((n,)),
            dma((cols,)), dma((cols,)),
            dma((n,)), dma((n,)),
            dma((cols,)), dma((cols,)),
            dma((cols, per)), dma((cols, per)),
            dma((cols,)),
        ],
        compiler_params=pltpu.CompilerParams(
            collective_id=0,
            has_side_effects=True,
            vmem_limit_bytes=(32 if n <= 16 else 61) * 2**20,
        ),
    )(tile_list, pair_list, occ_energy, vir_energy.reshape(-1, 64), amplitudes, lambdas)


def solution(mesh):
    return jax.shard_map(
        functools.partial(shards, mesh.shape["occ"]),
        mesh=mesh,
        in_specs=(
            P(("mol", "occ"), None, None, None),
            P(("mol", "occ"), None, None, None),
            P(("mol", "occ"), None),
            P(),
            P("mol"),
            P("mol"),
        ),
        out_specs=P(("mol", "occ"), None, None, None),
        check_vma=False,
    )
```

time: 182 us -> 87.3 us (0.48)
  Pallas kernels: 0 us -> 79.5 us
  blocking collectives: 63 us -> 0 us
  waiting for transfers between devices: 54.4 us -> 0 us
  local copies, waits for them, and re-layouts: 38.9 us -> 7.47 us
  starting transfers between devices: 18 us -> 0 us
  other arithmetic: 3.86 us -> 0 us
    pallas_call x0 -> x1, Pallas kernels: none -> 79.5 us  [shards(): pl.pallas_call(functools.partial(kernel, n, groups, nt), out_shape=jax.Sh...]
    psum x1 -> x0, blocking collectives: 63 us -> none  [shards(): intersection = lax.psum(partial_intersection, 'occ')]
    all_to_all x3 -> x0, waiting for transfers between devices: 54.4 us -> none  [the longest x1 21 us: shards(): lax.all_to_all(ladder, 'occ', split_axis=0, concat_axis=1, tiled=True)]
    all_to_all x3 -> x0, starting transfers between devices: 18 us -> none  [the longest x1 7.39 us: shards(): lax.all_to_all(amplitudes, 'occ', split_axis=1, concat_axis=0, tiled=True)]
    unnamed x21 -> x9, local copies, waits for them, and re-layouts: 23.8 us -> 6.69 us
    reshape x4 -> x1, local copies, waits for them, and re-layouts: 9.68 us -> 0.78 us  [shards(): vir_energy.reshape(-1, 64)]
    all_to_all x2 -> x0, local copies, waits for them, and re-layouts: 3.18 us -> none  [the longest x1 1.59 us: shards(): lax.all_to_all(amplitudes, 'occ', split_axis=1, concat_axis=0, tiled=True)]
    convert_element_type x1 -> x0, other arithmetic: 2.85 us -> none  [finish_update(): return (total / denom).astype(jnp.bfloat16)]
  transfers between devices with their start and end apart: 3 -> 0, of which waited for: 3 -> 0; matrix products, arithmetic and copies ran while one was open for 8% -> 0% of each run, Pallas kernels for 0% -> 0%
where the time goes in v1:
time: 87.3 us; the launch traced here: 87 us
  Pallas kernels  79.5 us (91%)
  local copies, waits for them, and re-layouts  7.47 us (9%)
    pallas_call x1, Pallas kernels, shards(): pl.pallas_call(functools.partial(kernel, n, groups, nt), out_shape=jax.Sh...  79.5 us
    unnamed x9, local copies, waits for them, and re-layouts  6.69 us

profile of v1, /device:TPU:0, one launch (start us, length us, event | category | flops | bytes accessed | tf_op | source)
XLA Modules:
  0.0 87.0 jit_solution(1289160443417430339)
XLA Ops:
  0.0 0.8 copy.8.pairs_ref
  0.8 0.8 copy.7.tiles_ref
  1.5 0.8 reshape.3.vir_ref
  2.3 0.0 copy-start
  2.3 1.6 %copy-done = bf16[8,16,64,64]{3,2,1,0:T(8,128)(2,1)S(1)} copy-done((bf16[8,16,64,64]{3,2,1,0:T(8,128)(2,1)S(1)}, bf16[8,16,64,64]{3,2,1,0:T(8,128)(2,1)}, u32[]{:S(2)}) %copy-start) | copy-done | bytes 1048600
  3.9 0.0 copy-start.1
  3.9 1.6 %copy-done.1 = bf16[8,16,64,64]{3,2,1,0:T(8,128)(2,1)S(1)} copy-done((bf16[8,16,64,64]{3,2,1,0:T(8,128)(2,1)S(1)}, bf16[8,16,64,64]{3,2,1,0:T(8,128)(2,1)}, u32[]{:S(2)}) %copy-start.1) | copy-done | bytes 1048600
  5.5 0.0 copy-start.2
  5.5 0.7 copy-done.2
  6.2 79.5 %shard_map.64 = bf16[8,16,64,64]{3,2,1,0:T(8,128)(2,1)S(1)} custom-call(s32[16,2]{1,0:T(8,128)S(1)} %copy.7.tiles_ref, s32[8,2]{1,0:T(8,128)S(1)} %copy.8.pairs_ref, f32[300]{0:T(512)S(1)} %copy-done.2, f32[38,64]{1,0:T(8,128)S(1)} %reshape.3.vir_ref, bf16[8,16,64,64]{3,2,1,0:T(8,128)(2,1)S(1)} %copy-done, bf16[8,16,64,64]{3,2,1,0:T(8,128)(2,1)S(1)} %copy-done.1), custom_call_target="tpu_custom_call" | custom-call | tf_op jit(solution)/shard_map/pallas_call | solution.py:296
  85.7 1.3 %copy.10 = bf16[8,16,64,64]{3,2,1,0:T(8,128)(2,1)} copy(bf16[8,16,64,64]{3,2,1,0:T(8,128)(2,1)S(1)} %shard_map.64) | data formatting | bytes 2097152
Async XLA Ops:
  2.3 1.6 %copy-start = (bf16[8,16,64,64]{3,2,1,0:T(8,128)(2,1)S(1)}, bf16[8,16,64,64]{3,2,1,0:T(8,128)(2,1)}, u32[]{:S(2)}) copy-start(bf16[8,16,64,64]{3,2,1,0:T(8,128)(2,1)} %amp_hbm.1) | copy-start | bytes 3145732
  3.9 1.6 %copy-start.1 = (bf16[8,16,64,64]{3,2,1,0:T(8,128)(2,1)S(1)}, bf16[8,16,64,64]{3,2,1,0:T(8,128)(2,1)}, u32[]{:S(2)}) copy-start(bf16[8,16,64,64]{3,2,1,0:T(8,128)(2,1)} %lam_hbm.1) | copy-start | bytes 3145732
  5.5 0.7 copy-start.2

commit v2 on v1

v2 whole, which is shorter than its diff:
```python
import functools

import jax
import jax.numpy as jnp
from jax import lax
from jax.experimental import pallas as pl
from jax.experimental.pallas import tpu as pltpu
from jax.sharding import PartitionSpec as P

F32 = jnp.float32
BF16 = jnp.bfloat16
HELD = 8
ROWS = 256
FOLD = 32


def fold_tile(x):
    return jnp.concatenate([x[:, :FOLD, :], x[:, FOLD:, :]], axis=-1)


def kernel(
    n, groups, nt,
    tiles_ref, pairs_ref, occ_ref, vir_ref, amp_hbm, lam_hbm,
    out_hbm,
    amp, lam, pt, plam, lamh, tbuf, lbuf, lad, ladr, dscr, gacc, asend, arecv, bsend, brecv, kmat,
    in_sem, t_send, t_recv, l_send, l_recv, a_send, a_recv, b_send, b_recv, d_send, d_recv, o_sem,
):
    cols = n // groups
    per = nt // cols
    me = lax.axis_index("occ")
    c = me % cols
    first = (me // cols) * cols

    def chunk(k):
        return lax.rem(c + k, cols)

    def load(which, src, dst, s):
        return pltpu.make_async_copy(src.at[:, s], dst.at[:, s], in_sem.at[which, s])

    def load_start(k, _):
        s = chunk(k % cols) * per + k // cols
        load(0, amp_hbm, amp, s).start()
        load(1, lam_hbm, lam, s).start()
        return 0

    lax.fori_loop(0, nt, load_start, 0)

    barrier = pltpu.get_barrier_semaphore()

    def greet(k, _):
        pl.semaphore_signal(
            barrier, inc=1, device_id={"occ": lax.rem(me + k, n)}, device_id_type=pl.DeviceIdType.MESH
        )
        return 0

    lax.fori_loop(1, n, greet, 0)

    r_id = lax.broadcasted_iota(jnp.int32, (ROWS, ROWS), 0)
    m_id = lax.broadcasted_iota(jnp.int32, (ROWS, ROWS), 1)
    pack_m = ((r_id % HELD) * FOLD + r_id // HELD == m_id).astype(BF16)
    unpack_m = ((m_id % HELD) * FOLD + m_id // HELD == r_id).astype(BF16)

    def pack(s):
        load(0, amp_hbm, amp, s).wait()
        load(1, lam_hbm, lam, s).wait()
        t = fold_tile(amp[:, s]).reshape(ROWS, 2 * 64)
        pt[s] = jnp.dot(pack_m, t, preferred_element_type=F32).astype(BF16)
        u = fold_tile(lam[:, s]).reshape(ROWS, 2 * 64)
        lamh[s] = u
        plam[s] = jnp.dot(pack_m, u, preferred_element_type=F32).astype(BF16)

    def rcopy(src, dst, send, recv, peer):
        return pltpu.make_async_remote_copy(
            src_ref=src, dst_ref=dst, send_sem=send, recv_sem=recv,
            device_id={"occ": peer}, device_id_type=pl.DeviceIdType.MESH,
        )

    def send_t(peer, t):
        s = lax.rem(peer, cols) * per + t
        return rcopy(pt.at[s], tbuf.at[me, t], t_send.at[peer, t], t_recv.at[me, t], peer)

    def send_l(cc, t):
        s = cc * per + t
        return rcopy(plam.at[s], lbuf.at[c, t], l_send.at[cc, t], l_recv.at[c, t], first + cc)

    def wait_t(src, t):
        rcopy(pt.at[0], tbuf.at[src, t], t_send.at[src, t], t_recv.at[src, t], src).wait_recv()

    def wait_l(cc, t):
        rcopy(plam.at[0], lbuf.at[cc, t], l_send.at[cc, t], l_recv.at[cc, t], first + cc).wait_recv()

    pack(c * per)
    pl.semaphore_wait(barrier, n - 1)
    for t in range(per):
        if t > 0:
            pack(c * per + t)
        for g in range(1, groups):
            send_t(lax.rem(me + g * cols, n), t).start()

        def pack_send(k, _):
            cc = chunk(k)
            pack(cc * per + t)
            for g in range(groups - 1, -1, -1):
                send_t(lax.rem(first + g * cols, n) + cc, t).start()
            send_l(cc, t).start()
            return 0

        lax.fori_loop(1, cols, pack_send, 0)
    tbuf[me] = pt[pl.ds(c * per, per)]
    lbuf[c] = plam[pl.ds(c * per, per)]

    def vir_tile(i):
        row = vir_ref[pl.ds(i // 2, 1), :]
        return jnp.where(i % 2 == 0, row[:, :64], row[:, 64:])

    def energies(s, _):
        one = vir_tile(tiles_ref[0, s])
        two = vir_tile(tiles_ref[1, s])
        d = jnp.transpose(jnp.broadcast_to(one, (64, 64))) + two
        dscr[s] = jnp.concatenate([d[:FOLD], d[FOLD:]], axis=-1)
        return 0

    lax.fori_loop(0, nt, energies, 0)

    def two_rows(ref, lo, count, t, g):
        a = ref[pl.ds(lo, count), t, pl.ds(g * 32, 16), :].reshape(count * 16, 128)
        b = ref[pl.ds(lo, count), t, pl.ds(g * 32 + 16, 16), :].reshape(count * 16, 128)
        return jnp.concatenate([a, b], axis=-1)

    for t in range(per):
        def arrive_t(k, _):
            wait_t(lax.rem(me + n - k, n), t)
            return 0

        def arrive_l(k, _):
            wait_l(lax.rem(c + cols - k, cols), t)
            return 0

        lax.fori_loop(1, cols, arrive_l, 0)
        lax.fori_loop(1, n, arrive_t, 0)

        def gram(i, _):
            acc = None
            for g in range(ROWS // 32):
                x = two_rows(tbuf, i * 16, 16, t, g)
                y = two_rows(lbuf, 0, cols, t, g)
                term = lax.dot_general(x, y, (((1,), (1,)), ((), ())), preferred_element_type=F32)
                acc = term if acc is None else acc + term
            rows = pl.ds(i * 256, 256)
            gacc[rows, :] = acc if t == 0 else gacc[rows, :] + acc
            return 0

        lax.fori_loop(0, n // 16, gram, 0)

    width = cols * 16
    odd = (lax.broadcasted_iota(jnp.int32, (HELD, width), 1) // HELD) % 2

    def fold_gram(i, _):
        lo = gacc[pl.ds(i * 16, HELD), :]
        hi = gacc[pl.ds(i * 16 + HELD, HELD), :]
        asend[i] = jnp.where(odd == 0, lo, hi)
        return 0

    lax.fori_loop(0, n, fold_gram, 0, unroll=4)

    def send_a(peer):
        return rcopy(asend.at[peer], arecv.at[me], a_send.at[peer], a_recv.at[me], peer)

    def start_a(k, _):
        send_a(lax.rem(me + k, n)).start()
        return 0

    lax.fori_loop(1, n, start_a, 0)
    arecv[me] = asend[me]

    def arrive_a(k, _):
        src = lax.rem(me + n - k, n)
        rcopy(asend.at[src], arecv.at[src], a_send.at[src], a_recv.at[src], src).wait_recv()
        return 0

    lax.fori_loop(1, n, arrive_a, 0)
    for g in range(groups):
        total = arecv[g * cols]
        for i in range(1, cols):
            total = total + arecv[g * cols + i]
        other = jnp.where(odd == 0, pltpu.roll(total, width - HELD, 1), pltpu.roll(total, HELD, 1))
        rounded = (total + other).astype(BF16).astype(F32)
        bsend[:, g * width:(g + 1) * width] = 0.5 * rounded

    def send_b(cc):
        return rcopy(bsend, brecv.at[c], b_send.at[cc], b_recv.at[c], first + cc)

    def start_b(k, _):
        send_b(chunk(k)).start()
        return 0

    lax.fori_loop(1, cols, start_b, 0)
    brecv[c] = bsend[...]

    def arrive_b(k, _):
        cc = lax.rem(c + cols - k, cols)
        rcopy(bsend, brecv.at[cc], b_send.at[cc], b_recv.at[cc], first + cc).wait_recv()
        return 0

    lax.fori_loop(1, cols, arrive_b, 0)
    all_odd = (lax.broadcasted_iota(jnp.int32, (HELD, n * 16), 1) // HELD) % 2

    def expand(i, _):
        rows = brecv[i]
        both = jnp.concatenate(
            [jnp.where(all_odd == 0, rows, 0.0), jnp.where(all_odd == 1, rows, 0.0)], axis=0
        )
        kmat[pl.ds(i * 16, 16), :] = both.astype(BF16)
        return 0

    lax.fori_loop(0, cols, expand, 0, unroll=8)

    def send_d(cc, t):
        return rcopy(lad.at[cc, t], ladr.at[c, t], d_send.at[cc, t], d_recv.at[c, t], first + cc)

    for t in range(per):
        def ladder(g, _):
            x = two_rows(tbuf, 0, n, t, g)
            y = jnp.dot(kmat[...], x, preferred_element_type=F32).astype(BF16)
            lad[:, t, pl.ds(g * 32, 16), :] = y[:, :128].reshape(cols, 16, 128)
            lad[:, t, pl.ds(g * 32 + 16, 16), :] = y[:, 128:].reshape(cols, 16, 128)
            return 0

        lax.fori_loop(0, ROWS // 32, ladder, 0, unroll=8 if n <= 16 else 1)

        def start_d(k, _):
            send_d(chunk(k), t).start()
            return 0

        lax.fori_loop(1, cols, start_d, 0)
    ladr[c] = lad[c]

    def drain_n(k, _):
        peer = lax.rem(me + k, n)
        for t in range(per):
            send_t(peer, t).wait_send()
        send_a(peer).wait_send()
        return 0

    def drain_c(k, _):
        cc = chunk(k)
        for t in range(per):
            send_l(cc, t).wait_send()
        send_b(cc).wait_send()
        return 0

    def store(s):
        return pltpu.make_async_copy(amp.at[:, s], out_hbm.at[:, s], o_sem.at[s])

    def finish(cc, t):
        s = cc * per + t
        z = jnp.dot(unpack_m, ladr[cc, t], preferred_element_type=F32)
        total = lamh[s].astype(F32) + z
        d = dscr[s]
        for p in range(HELD):
            e = d - occ_ref[pairs_ref[0, p]] - occ_ref[pairs_ref[1, p]]
            q = total[p * FOLD:(p + 1) * FOLD] / e
            amp[p, s, :FOLD, :] = q[:, :64].astype(BF16)
            amp[p, s, FOLD:, :] = q[:, 64:].astype(BF16)
        store(s).start()

    for t in range(per):
        finish(c, t)
    lax.fori_loop(1, n, drain_n, 0)
    lax.fori_loop(1, cols, drain_c, 0)
    for t in range(per):
        def arrive_d(k, _):
            cc = lax.rem(c + cols - k, cols)
            rcopy(
                lad.at[cc, t], ladr.at[cc, t], d_send.at[cc, t], d_recv.at[cc, t], first + cc
            ).wait_recv()
            finish(cc, t)
            return 0

        lax.fori_loop(1, cols, arrive_d, 0)

    def drain_d(k, _):
        for t in range(per):
            send_d(chunk(k), t).wait_send()
        return 0

    lax.fori_loop(1, cols, drain_d, 0)

    def drain_out(s, _):
        store(s).wait()
        return 0

    lax.fori_loop(0, nt, drain_out, 0)


def shards(n, amplitudes, lambdas, pair_list, tile_list, occ_energy, vir_energy):
    nt = amplitudes.shape[1]
    groups = 2
    cols = n // groups
    per = nt // cols
    packed = (nt, ROWS, 128)
    dma = pltpu.SemaphoreType.DMA
    smem = pl.BlockSpec(memory_space=pltpu.SMEM)
    vmem = pl.BlockSpec(memory_space=pltpu.VMEM)
    hbm = pl.BlockSpec(memory_space=pltpu.HBM)
    return pl.pallas_call(
        functools.partial(kernel, n, groups, nt),
        out_shape=jax.ShapeDtypeStruct(lambdas.shape, BF16),
        in_specs=[smem, smem, smem, vmem, hbm, hbm],
        out_specs=pl.BlockSpec(memory_space=pl.ANY),
        scratch_shapes=[
            pltpu.VMEM(amplitudes.shape, BF16),
            pltpu.VMEM(lambdas.shape, BF16),
            pltpu.VMEM(packed, BF16),
            pltpu.VMEM(packed, BF16),
            pltpu.VMEM(packed, BF16),
            pltpu.VMEM((n, per, ROWS, 128), BF16),
            pltpu.VMEM((cols, per, ROWS, 128), BF16),
            pltpu.VMEM((cols, per, ROWS, 128), BF16),
            pltpu.VMEM((cols, per, ROWS, 128), BF16),
            pltpu.VMEM((nt, FOLD, 128), F32),
            pltpu.VMEM((n * 16, cols * 16), F32),
            pltpu.VMEM((n, HELD, cols * 16), F32),
            pltpu.VMEM((n, HELD, cols * 16), F32),
            pltpu.VMEM((HELD, n * 16), F32),
            pltpu.VMEM((cols, HELD, n * 16), F32),
            pltpu.VMEM((cols * 16, n * 16), BF16),
            dma((2, nt)),
            dma((n, per)), dma((n, per)),
            dma((cols, per)), dma((cols, per)),
            dma((n,)), dma((n,)),
            dma((cols,)), dma((cols,)),
            dma((cols, per)), dma((cols, per)),
            dma((nt,)),
        ],
        compiler_params=pltpu.CompilerParams(
            collective_id=0,
            has_side_effects=True,
            vmem_limit_bytes=61 * 2**20,
        ),
    )(tile_list.T, pair_list.T, occ_energy, vir_energy.reshape(-1, 128), amplitudes, lambdas)


def solution(mesh):
    return jax.shard_map(
        functools.partial(shards, mesh.shape["occ"]),
        mesh=mesh,
        in_specs=(
            P(("mol", "occ"), None, None, None),
            P(("mol", "occ"), None, None, None),
            P(("mol", "occ"), None),
            P(),
            P("mol"),
            P("mol"),
        ),
        out_specs=P(("mol", "occ"), None, None, None),
        check_vma=False,
    )
```

time: 87.3 us -> 81.3 us (0.931)
  local copies, waits for them, and re-layouts: 7.47 us -> 3.08 us
  Pallas kernels: 79.5 us -> 78 us
    unnamed x9 -> x1, local copies, waits for them, and re-layouts: 6.69 us -> 3.08 us
    pallas_call x1, Pallas kernels: 79.5 us -> 78 us  [shards(): pl.pallas_call(functools.partial(kernel, n, groups, nt), out_shape=jax.Sh...]
where the time goes in v2:
time: 81.3 us; the launch traced here: 81.1 us
  Pallas kernels  78 us (96%)
  local copies, waits for them, and re-layouts  3.08 us (4%)
    pallas_call x1, Pallas kernels, shards(): pl.pallas_call(functools.partial(kernel, n, groups, nt), out_shape=jax.Sh...  78 us
    unnamed x1, local copies, waits for them, and re-layouts  3.08 us

profile of v2, /device:TPU:0, one launch (start us, length us, event | category | flops | bytes accessed | tf_op | source)
XLA Modules:
  0.0 81.1 jit_solution(16193489367805223563)
XLA Ops:
  0.0 78.0 %shard_map.64 = bf16[8,16,64,64]{3,2,1,0:T(8,128)(2,1)} custom-call(s32[2,16]{1,0:T(2,128)} %bitcast.4, s32[2,8]{1,0:T(2,128)} %bitcast.5, f32[300]{0:T(512)} %occ_ref.1, f32[19,128]{1,0:T(8,128)} %bitcast.3, bf16[8,16,64,64]{3,2,1,0:T(8,128)(2,1)} %amp_hbm.1, bf16[8,16,64,64]{3,2,1,0:T(8,128)(2,1)} %lam_hbm.1), custom_call_target="tpu_custom_call" | custom-call | tf_op jit(solution)/shard_map/pallas_call | solution.py:306
  78.0 3.1 %copy.8 = bf16[8,16,64,64]{3,2,1,0:T(8,128)(2,1)} copy(bf16[8,16,64,64]{3,2,1,0:T(8,128)(2,1)} %shard_map.64) | data formatting | bytes 2097152

commit v3 on v2

--- a/solution.py
+++ b/solution.py
@@ -22,8 +22,8 @@
     n, groups, nt,
     tiles_ref, pairs_ref, occ_ref, vir_ref, amp_hbm, lam_hbm,
     out_hbm,
-    amp, lam, pt, plam, lamh, tbuf, lbuf, lad, ladr, dscr, gacc, asend, arecv, bsend, brecv, kmat,
-    in_sem, t_send, t_recv, l_send, l_recv, a_send, a_recv, b_send, b_recv, d_send, d_recv, o_sem,
+    amp, lam, pt, plam, lamh, tbuf, lbuf, ladr, dscr, gacc, asend, arecv, brecv, kmat,
+    in_sem, t_send, t_recv, l_send, l_recv, a_send, a_recv, d_send, d_recv, o_sem,
 ):
     cols = n // groups
     per = nt // cols
@@ -155,54 +155,52 @@
     width = cols * 16
     odd = (lax.broadcasted_iota(jnp.int32, (HELD, width), 1) // HELD) % 2
 
-    def fold_gram(i, _):
-        lo = gacc[pl.ds(i * 16, HELD), :]
-        hi = gacc[pl.ds(i * 16 + HELD, HELD), :]
-        asend[i] = jnp.where(odd == 0, lo, hi)
-        return 0
-
-    lax.fori_loop(0, n, fold_gram, 0, unroll=4)
+    def swap(v):
+        return jnp.where(odd == 0, pltpu.roll(v, width - HELD, 1), pltpu.roll(v, HELD, 1))
+
+    def block(i):
+        v = jnp.where(odd == 0, gacc[pl.ds(i * 16, HELD), :], gacc[pl.ds(i * 16 + HELD, HELD), :])
+        return v + swap(v)
+
+    for g in range(groups):
+        def fold_gram(m, _):
+            i = g * cols + 4 * m
+            v = jnp.concatenate(
+                [jnp.where(odd == 0, block(i + j), block(i + j + 1)) for j in (0, 2)], axis=0
+            )
+            asend[g, pl.ds(m * 16, 16), :] = v.astype(BF16)
+            return 0
+
+        lax.fori_loop(0, cols // 4, fold_gram, 0, unroll=2)
 
     def send_a(peer):
-        return rcopy(asend.at[peer], arecv.at[me], a_send.at[peer], a_recv.at[me], peer)
+        return rcopy(asend.at[peer // cols], arecv.at[me], a_send.at[peer], a_recv.at[me], peer)
 
     def start_a(k, _):
         send_a(lax.rem(me + k, n)).start()
         return 0
 
     lax.fori_loop(1, n, start_a, 0)
-    arecv[me] = asend[me]
+    arecv[me] = asend[me // cols]
 
     def arrive_a(k, _):
         src = lax.rem(me + n - k, n)
-        rcopy(asend.at[src], arecv.at[src], a_send.at[src], a_recv.at[src], src).wait_recv()
+        rcopy(asend.at[0], arecv.at[src], a_send.at[src], a_recv.at[src], src).wait_recv()
         return 0
 
     lax.fori_loop(1, n, arrive_a, 0)
     for g in range(groups):
-        total = arecv[g * cols]
+        lanes = slice(g * width, (g + 1) * width)
+        total = arecv[g * cols].astype(F32)
         for i in range(1, cols):
-            total = total + arecv[g * cols + i]
-        other = jnp.where(odd == 0, pltpu.roll(total, width - HELD, 1), pltpu.roll(total, HELD, 1))
-        rounded = (total + other).astype(BF16).astype(F32)
-        bsend[:, g * width:(g + 1) * width] = 0.5 * rounded
-
-    def send_b(cc):
-        return rcopy(bsend, brecv.at[c], b_send.at[cc], b_recv.at[c], first + cc)
-
-    def start_b(k, _):
-        send_b(chunk(k)).start()
-        return 0
-
-    lax.fori_loop(1, cols, start_b, 0)
-    brecv[c] = bsend[...]
-
-    def arrive_b(k, _):
-        cc = lax.rem(c + cols - k, cols)
-        rcopy(bsend, brecv.at[cc], b_send.at[cc], b_recv.at[cc], first + cc).wait_recv()
-        return 0
-
-    lax.fori_loop(1, cols, arrive_b, 0)
+            total = total + arecv[g * cols + i].astype(F32)
+        total = 0.5 * total.astype(BF16).astype(F32)
+        for j in range(cols // 2):
+            v = total[j * HELD:(j + 1) * HELD]
+            w = swap(v)
+            brecv[2 * j, :, lanes] = jnp.where(odd == 0, v, w)
+            brecv[2 * j + 1, :, lanes] = jnp.where(odd == 0, w, v)
+
     all_odd = (lax.broadcasted_iota(jnp.int32, (HELD, n * 16), 1) // HELD) % 2
 
     def expand(i, _):
@@ -215,6 +213,8 @@
 
     lax.fori_loop(0, cols, expand, 0, unroll=8)
 
+    lad = lbuf
+
     def send_d(cc, t):
         return rcopy(lad.at[cc, t], ladr.at[c, t], d_send.at[cc, t], d_recv.at[c, t], first + cc)
 
@@ -246,7 +246,6 @@
         cc = chunk(k)
         for t in range(per):
             send_l(cc, t).wait_send()
-        send_b(cc).wait_send()
         return 0
 
     def store(s):
@@ -317,19 +316,16 @@
             pltpu.VMEM((n, per, ROWS, 128), BF16),
             pltpu.VMEM((cols, per, ROWS, 128), BF16),
             pltpu.VMEM((cols, per, ROWS, 128), BF16),
-            pltpu.VMEM((cols, per, ROWS, 128), BF16),
             pltpu.VMEM((nt, FOLD, 128), F32),
             pltpu.VMEM((n * 16, cols * 16), F32),
-            pltpu.VMEM((n, HELD, cols * 16), F32),
-            pltpu.VMEM((n, HELD, cols * 16), F32),
-            pltpu.VMEM((HELD, n * 16), F32),
+            pltpu.VMEM((groups, cols * 4, cols * 16), BF16),
+            pltpu.VMEM((n, cols * 4, cols * 16), BF16),
             pltpu.VMEM((cols, HELD, n * 16), F32),
             pltpu.VMEM((cols * 16, n * 16), BF16),
             dma((2, nt)),
             dma((n, per)), dma((n, per)),
             dma((cols, per)), dma((cols, per)),
             dma((n,)), dma((n,)),
-            dma((cols,)), dma((cols,)),
             dma((cols, per)), dma((cols, per)),
             dma((nt,)),
         ],

time: 81.3 us -> 78.8 us (0.969)
  Pallas kernels: 78 us -> 75.5 us
    pallas_call x1, Pallas kernels: 78 us -> 75.5 us  [shards(): pl.pallas_call(functools.partial(kernel, n, groups, nt), out_shape=jax.Sh...]
where the time goes in v3:
time: 78.8 us; the launch traced here: 78.6 us
  Pallas kernels  75.5 us (96%)
  local copies, waits for them, and re-layouts  3.08 us (4%)
    pallas_call x1, Pallas kernels, shards(): pl.pallas_call(functools.partial(kernel, n, groups, nt), out_shape=jax.Sh...  75.5 us
    unnamed x1, local copies, waits for them, and re-layouts  3.08 us

profile of v3, /device:TPU:0, one launch (start us, length us, event | category | flops | bytes accessed | tf_op | source)
XLA Modules:
  0.0 78.6 jit_solution(615978889732894585)
XLA Ops:
  0.0 75.5 %shard_map.64 = bf16[8,16,64,64]{3,2,1,0:T(8,128)(2,1)} custom-call(s32[2,16]{1,0:T(2,128)} %bitcast.4, s32[2,8]{1,0:T(2,128)} %bitcast.5, f32[300]{0:T(512)} %occ_ref.1, f32[19,128]{1,0:T(8,128)} %bitcast.3, bf16[8,16,64,64]{3,2,1,0:T(8,128)(2,1)} %amp_hbm.1, bf16[8,16,64,64]{3,2,1,0:T(8,128)(2,1)} %lam_hbm.1), custom_call_target="tpu_custom_call" | custom-call | tf_op jit(solution)/shard_map/pallas_call | solution.py:305
  75.5 3.1 %copy.8 = bf16[8,16,64,64]{3,2,1,0:T(8,128)(2,1)} copy(bf16[8,16,64,64]{3,2,1,0:T(8,128)(2,1)} %shard_map.64) | data formatting | bytes 2097152

commit v4 on v3

--- a/solution.py
+++ b/solution.py
@@ -20,10 +20,11 @@
 
 def kernel(
     n, groups, nt,
-    tiles_ref, pairs_ref, occ_ref, vir_ref, amp_hbm, lam_hbm,
+    tiles_hbm, pairs_hbm, occ_hbm, vir_hbm, amp_hbm, lam_hbm,
     out_hbm,
     amp, lam, pt, plam, lamh, tbuf, lbuf, ladr, dscr, gacc, asend, arecv, brecv, kmat,
     in_sem, t_send, t_recv, l_send, l_recv, a_send, a_recv, d_send, d_recv, o_sem,
+    tiles_ref, pairs_ref, occ_ref, vir_ref, table_sem,
 ):
     cols = n // groups
     per = nt // cols
@@ -44,6 +45,14 @@
         return 0
 
     lax.fori_loop(0, nt, load_start, 0)
+    tables = [
+        pltpu.make_async_copy(src, dst, table_sem.at[i])
+        for i, (src, dst) in enumerate(
+            [(tiles_hbm, tiles_ref), (pairs_hbm, pairs_ref), (occ_hbm, occ_ref), (vir_hbm, vir_ref)]
+        )
+    ]
+    for copy in tables:
+        copy.start()
 
     barrier = pltpu.get_barrier_semaphore()
 
@@ -120,6 +129,8 @@
         dscr[s] = jnp.concatenate([d[:FOLD], d[FOLD:]], axis=-1)
         return 0
 
+    for copy in tables:
+        copy.wait()
     lax.fori_loop(0, nt, energies, 0)
 
     def two_rows(ref, lo, count, t, g):
@@ -299,13 +310,11 @@
     per = nt // cols
     packed = (nt, ROWS, 128)
     dma = pltpu.SemaphoreType.DMA
-    smem = pl.BlockSpec(memory_space=pltpu.SMEM)
-    vmem = pl.BlockSpec(memory_space=pltpu.VMEM)
     hbm = pl.BlockSpec(memory_space=pltpu.HBM)
     return pl.pallas_call(
         functools.partial(kernel, n, groups, nt),
         out_shape=jax.ShapeDtypeStruct(lambdas.shape, BF16),
-        in_specs=[smem, smem, smem, vmem, hbm, hbm],
+        in_specs=[hbm] * 6,
         out_specs=pl.BlockSpec(memory_space=pl.ANY),
         scratch_shapes=[
             pltpu.VMEM(amplitudes.shape, BF16),
@@ -328,6 +337,11 @@
             dma((n,)), dma((n,)),
             dma((cols, per)), dma((cols, per)),
             dma((nt,)),
+            pltpu.SMEM(tile_list.shape[::-1], jnp.int32),
+            pltpu.SMEM(pair_list.shape[::-1], jnp.int32),
+            pltpu.SMEM(occ_energy.shape, F32),
+            pltpu.VMEM((vir_energy.shape[0] // 128, 128), F32),
+            dma((4,)),
         ],
         compiler_params=pltpu.CompilerParams(
             collective_id=0,

time: 78.8 us -> 77.8 us (0.987)
  Pallas kernels: 75.5 us -> 74.6 us
    pallas_call x1, Pallas kernels: 75.5 us -> 74.6 us  [shards(): pl.pallas_call(functools.partial(kernel, n, groups, nt), out_shape=jax.Sh...]
where the time goes in v4:
time: 77.8 us; the launch traced here: 77.7 us
  Pallas kernels  74.6 us (96%)
  local copies, waits for them, and re-layouts  3.08 us (4%)
    pallas_call x1, Pallas kernels, shards(): pl.pallas_call(functools.partial(kernel, n, groups, nt), out_shape=jax.Sh...  74.6 us
    unnamed x1, local copies, waits for them, and re-layouts  3.08 us

profile of v4, /device:TPU:0, one launch (start us, length us, event | category | flops | bytes accessed | tf_op | source)
XLA Modules:
  0.0 77.7 jit_solution(12742205975538261916)
XLA Ops:
  0.0 74.6 %shard_map.64 = bf16[8,16,64,64]{3,2,1,0:T(8,128)(2,1)} custom-call(s32[2,16]{1,0:T(2,128)} %bitcast.4, s32[2,8]{1,0:T(2,128)} %bitcast.5, f32[300]{0:T(512)} %occ_hbm.1, f32[19,128]{1,0:T(8,128)} %bitcast.3, bf16[8,16,64,64]{3,2,1,0:T(8,128)(2,1)} %amp_hbm.1, bf16[8,16,64,64]{3,2,1,0:T(8,128)(2,1)} %lam_hbm.1), custom_call_target="tpu_custom_call" | custom-call | tf_op jit(solution)/shard_map/pallas_call | solution.py:314
  74.6 3.1 %copy.8 = bf16[8,16,64,64]{3,2,1,0:T(8,128)(2,1)} copy(bf16[8,16,64,64]{3,2,1,0:T(8,128)(2,1)} %shard_map.64) | data formatting | bytes 2097152
